TPU v7x, 512 devices: a whole 4x4x16 slice. The times are simulated.
512 devices in a mesh: dp: 16 (over z), expert: 32 (over x, y, core).
Axes of the slice: x: 4, y: 4, z: 16, core: 2. Of those that a mesh axis runs over, the one named last changes fastest.
Arguments:
- tokens: bfloat16 [65536, 1024], P(('dp', 'expert')), may hold values from -6 to 6
- route_ids: int32 [65536, 4], P(('dp', 'expert')), may hold values from 0 to 31, all different within a row; in each aligned block of 128 rows (0 to 127, 128 to 255, ...) at most 24 rows name the same one
- route_weights: float32 [65536, 4], P(('dp', 'expert')), may hold values from 0.2 to 1
- up_weight: bfloat16 [32, 1024, 704], P('expert', 'dp'), may hold values from -0.1875 to 0.1875
- down_weight: bfloat16 [32, 1024, 704], P('expert', 'dp'), may hold values from -0.21875 to 0.21875
- head_weight: bfloat16 [1024, 1024], P('dp'), may hold values from -0.75 to 0.75
- out_weight: float32 [1024], P('dp'), may hold values from -0.375 to 0.375
- pool_ids: int32 [512, 128], P(('dp', 'expert')), may hold values from 0 to 15, never falling along the last dimension, each value on 1 to 64 neighbouring positions
- list_ids: int32 [512, 16], P(('dp', 'expert')), may hold values from 0 to 7, as said below
- clicks: int32 [512, 16], P(('dp', 'expert')), may hold values 0 or 1
- ranks: int32 [512, 16], P(('dp', 'expert')), may hold values from 0 to 31
- alpha_table: float32 [32], replicated, may hold values from 0.3 to 1
- beta_table: float32 [32], replicated, may hold values from 0 to 0.3
Outputs:
- grad_up: bfloat16 [32, 1024, 704], P('expert', 'dp')
- grad_down: bfloat16 [32, 1024, 704], P('expert', 'dp')
- grad_head: float32 [1024, 1024], P('dp')
- grad_out: float32 [1024], P('dp')
- list_loss: float32 [32], P('expert')
Inputs may be any that keep to these rules, and one draw needn't show every extreme that they name: `route_ids`: each token names 4 different experts; among the 128 tokens of one device no expert is named more than 24 times, a bound that some block reaches. `pool_ids`: in each row the candidate number never falls, every candidate has 1 to 64 tokens and one has exactly 64. `list_ids`: every list number appears in every row.
All inputs are finite; a program needn't handle non-finite values. No bound on the sum of `clicks` on one device may be relied on, other than what follows from the above.
Results may differ from a plain program's by a relative error of at most 0.028.
Values may be sent and summed in bfloat16 or wider, within the bound.
A program may use at most 64 MiB of HBM per device.

v0:
```python
import jax
import jax.numpy as jnp
from jax import lax
from jax.sharding import PartitionSpec as P

LISTS = 8
RANKS = 32


def silu_slope(pre_act):
    sigmoid = jax.nn.sigmoid(pre_act)
    return sigmoid * (1.0 + pre_act * (1.0 - sigmoid))


def local(
    tokens,
    route_ids,
    route_weights,
    up_weight,
    down_weight,
    head_weight,
    out_weight,
    pool_ids,
    list_ids,
    clicks,
    ranks,
    alpha_table,
    beta_table,
):
    tok_count = tokens.shape[0]
    model_width = tokens.shape[1]
    top_count = route_ids.shape[1]
    owners = lax.axis_size("expert")
    capacity = 3 * tok_count * top_count // (2 * owners)
    slot_total = owners * capacity
    flat_ids = route_ids.reshape(-1)
    expert_hot = (flat_ids[:, None] == jnp.arange(owners, dtype=jnp.int32)[None, :]).astype(
        jnp.int32
    )
    running = jnp.cumsum(expert_hot, axis=0) - 1
    slot_index = jnp.sum(running * expert_hot, axis=1)
    target = flat_ids * capacity + slot_index
    token_index = jnp.arange(tok_count * top_count, dtype=jnp.int32) // top_count
    outgoing = (
        jnp.zeros((slot_total, model_width), jnp.bfloat16).at[target].set(tokens[token_index])
    )
    received = lax.all_to_all(
        outgoing.reshape(owners, capacity, model_width),
        "expert",
        split_axis=0,
        concat_axis=0,
        tiled=True,
    )
    inputs = received.reshape(slot_total, model_width)
    up_local = up_weight[0]
    down_local = down_weight[0]
    hidden_width = up_local.shape[1]
    columns = inputs
    pre_act = jnp.dot(
        columns,
        lax.all_gather(up_local, "dp", axis=0, tiled=True),
        preferred_element_type=jnp.float32,
    )
    activated = jax.nn.silu(pre_act).astype(jnp.bfloat16)
    expert_out = lax.dot_general(
        activated,
        lax.all_gather(down_local, "dp", axis=0, tiled=True),
        (((1,), (1,)), ((), ())),
        preferred_element_type=jnp.float32,
    ).astype(jnp.bfloat16)
    returned = lax.all_to_all(
        expert_out.reshape(owners, capacity, model_width),
        "expert",
        split_axis=0,
        concat_axis=0,
        tiled=True,
    ).reshape(slot_total, model_width)
    routed_rows = returned[target].reshape(tok_count, top_count, model_width)
    routed = jnp.sum(route_weights[:, :, None] * routed_rows.astype(jnp.float32), axis=1)
    mixed = tokens.astype(jnp.float32) + routed
    inv_rms = lax.rsqrt(jnp.mean(mixed * mixed, axis=1, keepdims=True) + 1e-06)
    normed = mixed * inv_rms
    cand_count = list_ids.shape[1]
    member = (pool_ids[0][:, None] == jnp.arange(cand_count, dtype=jnp.int32)[None, :]).astype(
        jnp.float32
    )
    token_counts = jnp.sum(member, axis=0)
    pooled_sum = lax.dot_general(
        member,
        normed,
        (((0,), (0,)), ((), ())),
        precision=lax.Precision.HIGHEST,
        preferred_element_type=jnp.float32,
    )
    pooled = (pooled_sum / token_counts[:, None]).astype(jnp.bfloat16)
    all_pooled = lax.all_gather(pooled, "dp", axis=0, tiled=True)
    head_act = jnp.tanh(
        lax.dot_general(
            all_pooled, head_weight, (((1,), (1,)), ((), ())), preferred_element_type=jnp.float32
        )
    )
    part_score = jnp.sum(head_act * out_weight[None, :], axis=1)
    rank_hot = (ranks[0][:, None] == jnp.arange(RANKS, dtype=jnp.int32)[None, :]).astype(
        jnp.float32
    )
    alpha_of = jnp.sum(rank_hot * alpha_table[None, :], axis=1)
    beta_of = jnp.sum(rank_hot * beta_table[None, :], axis=1)
    corrected = (clicks[0].astype(jnp.float32) - beta_of) / alpha_of
    list_hot = (list_ids[0][:, None] == jnp.arange(LISTS, dtype=jnp.int32)[None, :]).astype(
        jnp.float32
    )
    scores = lax.psum_scatter(part_score, "dp", scatter_dimension=0, tiled=True)
    exp_scores = jnp.exp(scores)
    exp_total, click_total, cross_total = lax.psum(
        (
            jnp.sum(exp_scores[:, None] * list_hot, axis=0),
            jnp.sum(corrected[:, None] * list_hot, axis=0),
            jnp.sum((corrected * scores)[:, None] * list_hot, axis=0),
        ),
        "dp",
    )
    list_loss = jnp.sum(click_total * jnp.log(exp_total) - cross_total).reshape(1)
    cand_grad = (
        jnp.sum(list_hot * (click_total / exp_total)[None, :], axis=1) * exp_scores - corrected
    )
    group_grad = lax.all_gather(cand_grad, "dp", axis=0, tiled=True)
    hid_grad = (group_grad[:, None] * out_weight[None, :] * (1.0 - head_act * head_act)).astype(
        jnp.bfloat16
    )
    head_term = lax.dot_general(
        hid_grad, all_pooled, (((0,), (0,)), ((), ())), preferred_element_type=jnp.float32
    )
    out_term = jnp.sum(group_grad[:, None] * head_act, axis=0)
    grad_head, grad_out = (
        lax.psum(head_term.astype(jnp.bfloat16), "expert").astype(jnp.float32),
        lax.psum(out_term.astype(jnp.bfloat16), "expert").astype(jnp.float32),
    )
    pooled_grad = lax.psum_scatter(
        jnp.dot(hid_grad, head_weight, preferred_element_type=jnp.float32).astype(jnp.bfloat16),
        "dp",
        scatter_dimension=0,
        tiled=True,
    ).astype(jnp.float32)
    normed_grad = jnp.dot(
        member,
        pooled_grad / token_counts[:, None],
        precision=lax.Precision.HIGHEST,
        preferred_element_type=jnp.float32,
    )
    mixed_grad = inv_rms * (
        normed_grad - normed * jnp.mean(normed_grad * normed, axis=1, keepdims=True)
    )
    cotangent = (
        (route_weights[:, :, None] * mixed_grad[:, None, :])
        .astype(jnp.bfloat16)
        .reshape(tok_count * top_count, model_width)
    )
    outgoing_grad = jnp.zeros((slot_total, model_width), jnp.bfloat16).at[target].set(cotangent)
    slot_grad = lax.all_to_all(
        outgoing_grad.reshape(owners, capacity, model_width),
        "expert",
        split_axis=0,
        concat_axis=0,
        tiled=True,
    ).reshape(slot_total, model_width)
    columns = slot_grad
    act_grad = jnp.dot(
        columns,
        lax.all_gather(down_local, "dp", axis=0, tiled=True),
        preferred_element_type=jnp.float32,
    )
    pre_grad = (act_grad * silu_slope(pre_act)).astype(jnp.bfloat16)
    up_term = lax.dot_general(
        inputs, pre_grad, (((0,), (0,)), ((), ())), preferred_element_type=jnp.float32
    )
    down_term = lax.dot_general(
        slot_grad, activated, (((0,), (0,)), ((), ())), preferred_element_type=jnp.float32
    )
    summed = lax.psum_scatter(
        jnp.concatenate([up_term, down_term], axis=1).astype(jnp.bfloat16),
        "dp",
        scatter_dimension=0,
        tiled=True,
    ).astype(jnp.float32)
    grad_up = summed[:, :hidden_width].astype(jnp.bfloat16)[None]
    grad_down = summed[:, hidden_width:].astype(jnp.bfloat16)[None]
    return (grad_up, grad_down, grad_head, grad_out, list_loss)


def solution(mesh):
    return jax.shard_map(
        local,
        mesh=mesh,
        in_specs=(
            P(("dp", "expert"), None),
            P(("dp", "expert"), None),
            P(("dp", "expert"), None),
            P("expert", "dp", None),
            P("expert", "dp", None),
            P("dp", None),
            P("dp"),
            P(("dp", "expert"), None),
            P(("dp", "expert"), None),
            P(("dp", "expert"), None),
            P(("dp", "expert"), None),
            P(),
            P(),
        ),
        out_specs=(
            P("expert", "dp", None),
            P("expert", "dp", None),
            P("dp", None),
            P("dp"),
            P("expert"),
        ),
        check_vma=False,
    )
```

profile of v0, /device:TPU:2, one launch (start us, length us, event | category | flops | bytes accessed | tf_op | source)
XLA Modules:
  0.0 616.2 jit_solution(5484869024064051022)
XLA Ops:
  10.6 1.2 reduce-window.6
  12.2 7.4 %scatter_custom_fusion = bf16[768,1024]{1,0:T(8,128)(2,1)S(1)} fusion(s32[512]{0:T(512)S(1)} %bitcast.67, bf16[128,1024]{1,0:T(8,128)(2,1)} %param.13, s32[1024]{0:T(1024)S(1)} %pad_clamp_fusion.1, bf16[]{:T(256)} %constant.40.clone.1), kind=kCustom, calls=%fused_computation.24 | custom fusion | bytes 1573376 | tf_op jit(solution)/shard_map/scatter | solution.py:45
  19.6 29.6 %all_to_all.15 = bf16[32,24,1024]{2,1,0:T(8,128)(2,1)S(1)} all-to-all(bf16[32,24,1024]{2,1,0:T(8,128)(2,1)S(1)} %bitcast.60), channel_id=1, replica_groups=mesh['dp'=16,'expert'=32] {'expert'}, dimensions={0} | all-to-all | bytes 3145728 | tf_op jit(solution)/shard_map/all_to_all | solution.py:47
  49.2 37.5 %all-gather.5.cloned.1.call-done = bf16[1,1024,704]{2,1,0:T(8,128)(2,1)} async-done(((bf16[1,64,704]{2,1,0:T(8,128)(2,1)}), bf16[1,1024,704]{2,1,0:T(8,128)(2,1)}) %all-gather.5.cloned.1.call-update) | async-done | bytes 1441808 | tf_op jit(solution)/shard_map/all_gather | solution.py:61
  86.7 4.1 fusion.2
  90.8 67.2 %all-gather.7.cloned.1.call-done = bf16[1,1024,704]{2,1,0:T(8,128)(2,1)} async-done(((bf16[1,64,704]{2,1,0:T(8,128)(2,1)}), bf16[1,1024,704]{2,1,0:T(8,128)(2,1)}) %all-gather.7.cloned.1.call-update) | async-done | bytes 1441808 | tf_op jit(solution)/shard_map/all_gather | solution.py:67
  158.0 4.7 convolution_convert_fusion
  162.7 7.6 %all-to-all-start.1 = ((bf16[32,24,1024]{2,1,0:T(8,128)(2,1)}), bf16[32,24,1024]{2,1,0:T(8,128)(2,1)S(1)}, u32[]{:S(2)}, u32[]{:S(2)}) async-start(bf16[32,24,1024]{2,1,0:T(8,128)(2,1)} %bitcast.8), calls=%async_computation.1 | async-start | bytes 3145728 | tf_op jit(solution)/shard_map/all_to_all | solution.py:71
  174.5 15.9 %all-to-all-done.1 = bf16[32,24,1024]{2,1,0:T(8,128)(2,1)S(1)} async-done(((bf16[32,24,1024]{2,1,0:T(8,128)(2,1)}), bf16[32,24,1024]{2,1,0:T(8,128)(2,1)S(1)}, u32[]{:S(2)}, u32[]{:S(2)}) %all-to-all-start.1) | async-done | bytes 1572896 | tf_op jit(solution)/shard_map/all_to_all | solution.py:71
  190.4 2.8 gather_fusion
  193.2 1.8 reshape.174
  195.0 1.3 multiply_reduce_fusion
  197.0 31.4 %all_gather.15 = bf16[256,1024]{1,0:T(8,128)(2,1)S(1)} all-gather(bf16[16,1024]{1,0:T(8,128)(2,1)S(1)} %fusion.4), channel_id=1, replica_groups=mesh['dp'=16,'expert'=32] {'dp'}, dimensions={0}, use_global_device_ids=true | all-gather | bytes 557056 | tf_op jit(solution)/shard_map/all_gather | solution.py:96
  228.7 27.0 %all-reduce.1 = f32[256]{0:T(256)S(1)} all-reduce(f32[256]{0:T(256)S(1)} %get-tuple-element.42), channel_id=4, replica_groups=mesh['dp'=16,'expert'=32] {'dp'}, use_global_device_ids=true, to_apply=%region_12.13.clone | all-reduce | flops 256 | bytes 2048
  256.0 29.0 %all-reduce.3 = (f32[8]{0:T(128)S(1)}, f32[8]{0:T(128)S(1)}) all-reduce(f32[8]{0:T(128)S(1)} %get-tuple-element.28, f32[8]{0:T(128)S(1)} %get-tuple-element.27), channel_id=1, replica_groups=mesh['dp'=16,'expert'=32] {'dp'}, use_global_device_ids=true, to_apply=%region_9.10 | all-reduce | flops 16 | bytes 128 | tf_op jit(solution)/shard_map/psum | solution.py:114
  285.2 27.6 %all-reduce.2 = (f32[256]{0:T(256)S(1)}, f32[8]{0:T(128)}) all-reduce(f32[256]{0:T(256)S(1)} %subtract_dynamic-update-slice_fusion, f32[8]{0:T(128)S(1)} %get-tuple-element.25), channel_id=1, replica_groups=mesh['dp'=16,'expert'=32] {'dp'}, use_global_device_ids=true, to_apply=%add | all-reduce | flops 264 | bytes 2112
  312.8 1.2 convolution_convert_fusion.3
  314.1 64.8 %reduce-scatter.5.cloned.1.call-done = bf16[16,1024]{1,0:T(8,128)(2,1)} async-done(((bf16[256,1024]{1,0:T(8,128)(2,1)}), bf16[16,1024]{1,0:T(8,128)(2,1)}) %reduce-scatter.5.cloned.1.call-update) | async-done | bytes 32784 | tf_op jit(solution)/shard_map/reduce_scatter | solution.py:138
  378.9 1.3 multiply_reduce_fusion.1
  380.4 1.9 mul.207
  382.3 2.0 mul.208
  384.3 3.9 scatter_custom_fusion.1
  388.2 7.5 %all-to-all-start.2 = ((bf16[32,24,1024]{2,1,0:T(8,128)(2,1)}), bf16[32,24,1024]{2,1,0:T(8,128)(2,1)S(1)}, u32[]{:S(2)}, u32[]{:S(2)}) async-start(bf16[32,24,1024]{2,1,0:T(8,128)(2,1)} %bitcast.59), calls=%async_computation.3 | async-start | bytes 3145728 | tf_op jit(solution)/shard_map/all_to_all | solution.py:159
  397.0 18.9 %all-to-all-done.2 = bf16[32,24,1024]{2,1,0:T(8,128)(2,1)S(1)} async-done(((bf16[32,24,1024]{2,1,0:T(8,128)(2,1)}), bf16[32,24,1024]{2,1,0:T(8,128)(2,1)S(1)}, u32[]{:S(2)}, u32[]{:S(2)}) %all-to-all-start.2) | async-done | bytes 1572896 | tf_op jit(solution)/shard_map/all_to_all | solution.py:159
  415.9 4.2 convolution_convert_fusion.1
  420.0 6.6 %convolution_convert_fusion.2 = bf16[1024,704]{0,1:T(8,128)(2,1)} fusion(bf16[768,1024]{1,0:T(8,128)(2,1)S(1)} %bitcast.62, f32[768,704]{0,1:T(8,128)} %fusion.2, bf16[768,1024]{1,0:T(8,128)(2,1)S(1)} %bitcast.64, bf16[1,1024,704]{2,1,0:T(8,128)(2,1)} %all-gather.7.cloned.1.call-done), kind=kOutput, calls=%fused_computation.12 | convolution fusion | flops 2220179456 | bytes 8192000 | tf_op jit(solution)/shard_map/dot_general | solution.py:173
  426.6 2.1 pad_maximum_fusion
  428.7 2.9 copy.45
  431.7 56.4 %psum.38 = bf16[64]{0:T(256)(128)(2,1)S(1)} all-reduce(bf16[64]{0:T(256)(128)(2,1)S(1)} %multiply_reduce_fusion.3), channel_id=1, replica_groups=mesh['dp'=16,'expert'=32] {'expert'}, use_global_device_ids=true, to_apply=%region_22.23 | all-reduce | flops 64 | bytes 256 | tf_op jit(solution)/shard_map/psum | solution.py:136
  489.2 39.0 %all-reduce.6.cloned.1.call-done = bf16[64,1024]{1,0:T(8,128)(2,1)} async-done(((bf16[64,1024]{1,0:T(8,128)(2,1)}), bf16[64,1024]{1,0:T(8,128)(2,1)}) %all-reduce.6.cloned.1.call-update) | async-done | bytes 131088 | tf_op jit(solution)/shard_map/psum | solution.py:135
  528.2 1.6 convert_element_type.86
  529.8 76.8 %reduce-scatter.7.cloned.1.call-done = bf16[64,1408]{1,0:T(8,128)(2,1)} async-done(((bf16[1024,1408]{1,0:T(8,128)(2,1)}), bf16[64,1408]{1,0:T(8,128)(2,1)}) %reduce-scatter.7.cloned.1.call-update) | async-done | bytes 180240
  (99 shorter events, 13.8 us)
Async XLA Ops:
  7.2 221.2 %copy-start = (bf16[64,1024]{1,0:T(8,128)(2,1)S(1)}, bf16[64,1024]{1,0:T(8,128)(2,1)}, u32[]{:S(2)}) copy-start(bf16[64,1024]{1,0:T(8,128)(2,1)} %param.18) | copy-start | bytes 393220
  7.2 79.5 %all-gather.5.cloned.1.call-start = ((), (), s32[]{:S(2)}) async-start(), calls=%async_computation.7 | async-start | bytes 1671168 | tf_op jit(solution)/shard_map/all_gather | solution.py:61
  7.9 150.1 %all-gather.7.cloned.1.call-start = ((), (), s32[]{:S(2)}) async-start(), calls=%async_computation.8 | async-start | bytes 1671168 | tf_op jit(solution)/shard_map/all_gather | solution.py:67
  49.2 41.6 %copy-start.2 = (bf16[32,24,1024]{2,1,0:T(8,128)(2,1)}, bf16[32,24,1024]{2,1,0:T(8,128)(2,1)S(1)}, u32[]{:S(2)}) copy-start(bf16[32,24,1024]{2,1,0:T(8,128)(2,1)S(1)} %all_to_all.15) | copy-start | bytes 4718596
  162.6 7.9 %copy-start.9 = (f32[128,4]{0,1:T(4,128)S(1)}, f32[128,4]{0,1:T(4,128)}, u32[]{:S(2)}) copy-start(f32[128,4]{0,1:T(4,128)} %param.15) | copy-start | bytes 6148
  162.6 8.6 %copy-start.16 = (u32[512]{0:T(512)S(1)}, u32[512]{0:T(512)}, u32[]{:S(2)}) copy-start(u32[512]{0:T(512)} %constant.64) | copy-start | bytes 6148
  162.6 10.5 %copy-start.12 = (s32[1,128]{1,0:T(1,128)S(1)}, s32[1,128]{1,0:T(1,128)}, u32[]{:S(2)}) copy-start(s32[1,128]{1,0:T(1,128)} %param.20) | copy-start | bytes 1540
  162.6 11.1 %copy-start.17 = (f32[32]{0:T(128)S(1)}, f32[32]{0:T(128)}, u32[]{:S(2)}) copy-start(f32[32]{0:T(128)} %param.25) | copy-start | bytes 388
  162.7 11.1 %copy-start.18 = (s32[1,16]{1,0:T(1,128)S(1)}, s32[1,16]{1,0:T(1,128)}, u32[]{:S(2)}) copy-start(s32[1,16]{1,0:T(1,128)} %param.23) | copy-start | bytes 196
  162.7 11.1 %copy-start.19 = (f32[32]{0:T(128)S(1)}, f32[32]{0:T(128)}, u32[]{:S(2)}) copy-start(f32[32]{0:T(128)} %param.24) | copy-start | bytes 388
  162.7 27.7 %all-to-all-start.1 = ((bf16[32,24,1024]{2,1,0:T(8,128)(2,1)}), bf16[32,24,1024]{2,1,0:T(8,128)(2,1)S(1)}, u32[]{:S(2)}, u32[]{:S(2)}) async-start(bf16[32,24,1024]{2,1,0:T(8,128)(2,1)} %bitcast.8), calls=%async_computation.1 | async-start | bytes 3145728 | tf_op jit(solution)/shard_map/all_to_all | solution.py:71
  170.3 208.6 %reduce-scatter.5.cloned.1.call-start = ((), (), s32[]{:S(2)}) async-start(), calls=%async_computation.5 | async-start | bytes 557056 | tf_op jit(solution)/shard_map/reduce_scatter | solution.py:138
  193.2 1.8 copy-start.6
  194.9 1.4 copy-start.1
  195.0 1.6 copy-start.14
  196.3 32.0 %copy-start.8 = (f32[64]{0:T(128)S(1)}, f32[64]{0:T(128)}, u32[]{:S(2)}) copy-start(f32[64]{0:T(128)} %param.19) | copy-start | bytes 772
  196.3 59.4 %copy-start.11 = (f32[16]{0:T(128)S(1)}, f32[16]{0:T(128)}, u32[]{:S(2)}) copy-start(f32[16]{0:T(128)} %get-tuple-element.30) | copy-start | bytes 196
  196.4 59.4 %copy-start.23 = (s32[1,16]{1,0:T(1,128)S(1)}, s32[1,16]{1,0:T(1,128)}, u32[]{:S(2)}) copy-start(s32[1,16]{1,0:T(1,128)} %param.22) | copy-start | bytes 196
  196.4 59.4 %copy-start.10 = (s32[1,16]{1,0:T(1,128)S(1)}, s32[1,16]{1,0:T(1,128)}, u32[]{:S(2)}) copy-start(s32[1,16]{1,0:T(1,128)} %param.21) | copy-start | bytes 196
  196.6 117.5 %copy-start.7 = (f32[128,4]{1,0:T(8,128)S(1)}, f32[128,4]{1,0:T(8,128)}, u32[]{:S(2)}) copy-start(f32[128,4]{1,0:T(8,128)} %copy.41) | copy-start | bytes 6148
  196.6 182.3 %copy-start.13 = (s32[1,128]{1,0:T(1,128)S(1)}, s32[1,128]{1,0:T(1,128)}, u32[]{:S(2)}) copy-start(s32[1,128]{1,0:T(1,128)} %param.20) | copy-start | bytes 1540
  196.6 182.3 %copy-start.15 = (f32[16]{0:T(128)S(1)}, f32[16]{0:T(128)}, u32[]{:S(2)}) copy-start(f32[16]{0:T(128)} %convert_reduce_fusion) | copy-start | bytes 196
  228.7 151.5 %copy-start.4 = (f32[256,64]{0,1:T(8,128)}, f32[256,64]{0,1:T(8,128)S(1)}, u32[]{:S(2)}) copy-start(f32[256,64]{0,1:T(8,128)S(1)} %get-tuple-element.43) | copy-start | bytes 196612
  285.0 95.4 %copy-start.20 = (f32[8]{0:T(128)}, f32[8]{0:T(128)S(1)}, u32[]{:S(2)}) copy-start(f32[8]{0:T(128)S(1)} %get-tuple-element.34) | copy-start | bytes 100
  388.2 7.6 %copy-start.5 = (f32[256,64]{0,1:T(8,128)S(1)}, f32[256,64]{0,1:T(8,128)}, u32[]{:S(2)}) copy-start(f32[256,64]{0,1:T(8,128)} %copy-done.4) | copy-start | bytes 196612
  388.2 27.7 %all-to-all-start.2 = ((bf16[32,24,1024]{2,1,0:T(8,128)(2,1)}), bf16[32,24,1024]{2,1,0:T(8,128)(2,1)S(1)}, u32[]{:S(2)}, u32[]{:S(2)}) async-start(bf16[32,24,1024]{2,1,0:T(8,128)(2,1)} %bitcast.59), calls=%async_computation.3 | async-start | bytes 3145728 | tf_op jit(solution)/shard_map/all_to_all | solution.py:159
  395.8 132.5 %all-reduce.6.cloned.1.call-start = ((), (), s32[]{:S(2)}) async-start(), calls=%async_computation.6 | async-start | bytes 262144 | tf_op jit(solution)/shard_map/psum | solution.py:135
  396.7 209.9 %reduce-scatter.7.cloned.1.call-start = ((), (), s32[]{:S(2)}) async-start(), calls=%async_computation.9 | async-start | bytes 3063808
  415.9 4.2 copy-start.3
  431.6 57.0 %copy-start.21 = (f32[8]{0:T(128)S(1)}, f32[8]{0:T(128)}, u32[]{:S(2)}) copy-start(f32[8]{0:T(128)} %copy-done.20) | copy-start | bytes 100
  431.6 57.0 %copy-start.22 = (f32[8]{0:T(128)S(1)}, f32[8]{0:T(128)}, u32[]{:S(2)}) copy-start(f32[8]{0:T(128)} %get-tuple-element.32) | copy-start | bytes 100
Sparse Core Ops, SparseCore 0:
  10.1 76.5 all-gather.4
  88.7 69.1 all-gather.6
  314.2 64.6 reduce-scatter.4
  400.4 127.7 all-reduce.5
  530.9 75.7 reduce-scatter.6
where the time goes:
time: 617 us; the launch traced here: 616 us
  waiting for transfers between devices  321 us (52%)
  blocking collectives  201 us (33%)
  local copies, waits for them, and re-layouts  24.7 us (4%)
  matrix products  23.6 us (4%)
  starting transfers between devices  15.7 us (3%)
  between operations  15.4 us (2%)
  other arithmetic  14.4 us (2%)
    unnamed x6, waiting for transfers between devices  78.3 us
    all_gather x1, waiting for transfers between devices, local(): lax.all_gather(down_local, 'dp', axis=0, tiled=True)  67.2 us
    reduce_scatter x1, waiting for transfers between devices, local(): lax.psum_scatter(jnp.dot(hid_grad, head_weight, preferred_element_type=jn...  64.8 us
    psum x1, blocking collectives, local(): lax.psum(out_term.astype(jnp.bfloat16), 'expert').astype(jnp.float32)  56.4 us
    unnamed x2, blocking collectives  54.6 us
    psum x1, waiting for transfers between devices, local(): lax.psum(head_term.astype(jnp.bfloat16), 'expert').astype(jnp.float32)  39 us
    all_gather x1, waiting for transfers between devices, local(): lax.all_gather(up_local, 'dp', axis=0, tiled=True)  37.5 us
    all_gather x1, blocking collectives, local(): all_pooled = lax.all_gather(pooled, 'dp', axis=0, tiled=True)  31.4 us
  transfers between devices with their start and end apart: 7, of which 7 were waited for; matrix products, arithmetic and copies ran while one was open for 6% of the time, Pallas kernels for 0%

commit v1 on v0

--- a/solution.py
+++ b/solution.py
@@ -93,7 +93,21 @@
         preferred_element_type=jnp.float32,
     )
     pooled = (pooled_sum / token_counts[:, None]).astype(jnp.bfloat16)
-    all_pooled = lax.all_gather(pooled, "dp", axis=0, tiled=True)
+    shares = lax.psum(1, "dp")
+    rack = [(k, (k + 1) % shares) for k in range(shares)]
+    opened, x_now = ([pooled], [pooled])
+    pages = [(k, (k - 1) % shares) for k in range(shares)]
+    for _ in range(shares // 2):
+        v_next = lax.ppermute(opened[-1], "dp", rack)
+        opened.append(v_next)
+    num = 0
+    while num < (shares - 1) // 2:
+        left_arr = lax.ppermute(x_now[-1], "dp", pages)
+        x_now.append(left_arr)
+        num += 1
+    local_part = jnp.concatenate([*opened[::-1], *x_now[1:]], axis=0)
+    spare = lax.axis_index("dp")
+    all_pooled = jnp.roll(local_part, (spare - shares // 2) * pooled.shape[0], axis=0)
     head_act = jnp.tanh(
         lax.dot_general(
             all_pooled, head_weight, (((1,), (1,)), ((), ())), preferred_element_type=jnp.float32

time: 617 us -> 651 us (1.055)
  starting transfers between devices: 15.7 us -> 68.5 us
  blocking collectives: 201 us -> 173 us
  waiting for transfers between devices: 321 us -> 328 us
    ppermute x0 -> x15, starting transfers between devices: none -> 52.8 us  [the longest x7 35.7 us: local(): left_arr = lax.ppermute(x_now[-1], 'dp', pages)]
    all_gather x1 -> x0, blocking collectives: 31.4 us -> none  [local(): all_pooled = lax.all_gather(pooled, 'dp', axis=0, tiled=True)]
  transfers between devices with their start and end apart: 7 -> 22, of which waited for: 7 -> 9; matrix products, arithmetic and copies ran while one was open for 6% -> 5% of each run, Pallas kernels for 0% -> 0%
where the time goes in v1:
time: 651 us; the launch traced here: 649 us
  waiting for transfers between devices  328 us (50%)
  blocking collectives  173 us (27%)
  starting transfers between devices  68.5 us (11%)
  local copies, waits for them, and re-layouts  27.1 us (4%)
  matrix products  23 us (4%)
  between operations  15.9 us (2%)
  other arithmetic  13.3 us (2%)
    unnamed x6, waiting for transfers between devices  78.3 us
    all_gather x1, waiting for transfers between devices, local(): lax.all_gather(down_local, 'dp', axis=0, tiled=True)  68.4 us
    reduce_scatter x1, waiting for transfers between devices, local(): lax.psum_scatter(jnp.dot(hid_grad, head_weight, preferred_element_type=jn...  65.2 us
    unnamed x2, blocking collectives  59.5 us
    psum x1, blocking collectives, local(): lax.psum(out_term.astype(jnp.bfloat16), 'expert').astype(jnp.float32)  56.4 us
    all_gather x1, waiting for transfers between devices, local(): lax.all_gather(up_local, 'dp', axis=0, tiled=True)  36.7 us
    psum x1, waiting for transfers between devices, local(): lax.psum(head_term.astype(jnp.bfloat16), 'expert').astype(jnp.float32)  36 us
    ppermute x7, starting transfers between devices, local(): left_arr = lax.ppermute(x_now[-1], 'dp', pages)  35.7 us
  transfers between devices with their start and end apart: 22, of which 9 were waited for; matrix products, arithmetic and copies ran while one was open for 5% of the time, Pallas kernels for 0%

profile of v1, /device:TPU:2, one launch (start us, length us, event | category | flops | bytes accessed | tf_op | source)
XLA Modules:
  0.0 649.3 jit_solution(18064722682112697466)
XLA Ops:
  12.2 7.4 %scatter_custom_fusion = bf16[768,1024]{1,0:T(8,128)(2,1)S(1)} fusion(s32[512]{0:T(512)S(1)} %bitcast.66, bf16[128,1024]{1,0:T(8,128)(2,1)} %param.13, s32[1024]{0:T(1024)S(1)} %pad_clamp_fusion.1, bf16[]{:T(256)} %constant.65.clone.1), kind=kCustom, calls=%fused_computation.24 | custom fusion | bytes 1573376 | tf_op jit(solution)/shard_map/scatter | solution.py:45
  19.6 30.3 %all_to_all.15 = bf16[32,24,1024]{2,1,0:T(8,128)(2,1)} all-to-all(bf16[32,24,1024]{2,1,0:T(8,128)(2,1)S(1)} %bitcast.58), channel_id=1, replica_groups=mesh['dp'=16,'expert'=32] {'expert'}, dimensions={0} | all-to-all | bytes 3145728 | tf_op jit(solution)/shard_map/all_to_all | solution.py:47
  49.9 36.7 %all-gather.5.cloned.1.call-done = bf16[1,1024,704]{2,1,0:T(8,128)(2,1)} async-done(((bf16[1,64,704]{2,1,0:T(8,128)(2,1)}), bf16[1,1024,704]{2,1,0:T(8,128)(2,1)}) %all-gather.5.cloned.1.call-update) | async-done | bytes 1441808 | tf_op jit(solution)/shard_map/all_gather | solution.py:61
  86.5 3.2 fusion.2
  89.8 68.4 %all-gather.7.cloned.1.call-done = bf16[1,1024,704]{2,1,0:T(8,128)(2,1)} async-done(((bf16[1,64,704]{2,1,0:T(8,128)(2,1)}), bf16[1,1024,704]{2,1,0:T(8,128)(2,1)}) %all-gather.7.cloned.1.call-update) | async-done | bytes 1441808 | tf_op jit(solution)/shard_map/all_gather | solution.py:67
  158.2 4.1 convolution_convert_fusion
  162.3 7.5 %all-to-all-start.1 = ((bf16[32,24,1024]{2,1,0:T(8,128)(2,1)}), bf16[32,24,1024]{2,1,0:T(8,128)(2,1)S(1)}, u32[]{:S(2)}, u32[]{:S(2)}) async-start(bf16[32,24,1024]{2,1,0:T(8,128)(2,1)} %bitcast.63), calls=%async_computation.1 | async-start | bytes 3145728 | tf_op jit(solution)/shard_map/all_to_all | solution.py:71
  170.3 19.6 %all-to-all-done.1 = bf16[32,24,1024]{2,1,0:T(8,128)(2,1)S(1)} async-done(((bf16[32,24,1024]{2,1,0:T(8,128)(2,1)}), bf16[32,24,1024]{2,1,0:T(8,128)(2,1)S(1)}, u32[]{:S(2)}, u32[]{:S(2)}) %all-to-all-start.1) | async-done | bytes 1572896 | tf_op jit(solution)/shard_map/all_to_all | solution.py:71
  189.9 2.8 gather_fusion
  196.4 3.4 collective-permute-start
  199.9 3.7 collective-permute-done
  203.6 2.1 collective-permute-start.1
  205.7 5.0 collective-permute-start.8
  212.6 5.1 collective-permute-start.9
  219.7 5.1 collective-permute-start.10
  226.8 5.1 collective-permute-start.11
  233.9 5.1 collective-permute-start.12
  241.0 5.1 collective-permute-start.13
  250.2 5.1 collective-permute-start.14
  258.4 30.5 %all-reduce.1 = f32[256]{0:T(256)S(1)} all-reduce(f32[256]{0:T(256)S(1)} %get-tuple-element.42), channel_id=4, replica_groups=mesh['dp'=16,'expert'=32] {'dp'}, use_global_device_ids=true, to_apply=%region_12.13.clone | all-reduce | flops 256 | bytes 2048
  289.2 27.0 %all-reduce.3 = (f32[8]{0:T(128)S(1)}, f32[8]{0:T(128)S(1)}) all-reduce(f32[8]{0:T(128)S(1)} %get-tuple-element.28, f32[8]{0:T(128)S(1)} %get-tuple-element.27), channel_id=1, replica_groups=mesh['dp'=16,'expert'=32] {'dp'}, use_global_device_ids=true, to_apply=%region_9.10 | all-reduce | flops 16 | bytes 128 | tf_op jit(solution)/shard_map/psum | solution.py:128
  316.5 29.0 %all-reduce.2 = (f32[256]{0:T(256)S(1)}, f32[8]{0:T(128)S(1)}) all-reduce(f32[256]{0:T(256)S(1)} %subtract_dynamic-update-slice_fusion, f32[8]{0:T(128)S(1)} %get-tuple-element.25), channel_id=1, replica_groups=mesh['dp'=16,'expert'=32] {'dp'}, use_global_device_ids=true, to_apply=%add | all-reduce | flops 264 | bytes 2112
  346.8 65.2 %reduce-scatter.5.cloned.1.call-done = bf16[16,1024]{1,0:T(8,128)(2,1)} async-done(((bf16[256,1024]{1,0:T(8,128)(2,1)}), bf16[16,1024]{1,0:T(8,128)(2,1)}) %reduce-scatter.5.cloned.1.call-update) | async-done | bytes 32784 | tf_op jit(solution)/shard_map/reduce_scatter | solution.py:152
  417.5 3.9 scatter_custom_fusion.1
  421.3 7.6 %all-to-all-start.2 = ((bf16[32,24,1024]{2,1,0:T(8,128)(2,1)}), bf16[32,24,1024]{2,1,0:T(8,128)(2,1)S(1)}, u32[]{:S(2)}, u32[]{:S(2)}) async-start(bf16[32,24,1024]{2,1,0:T(8,128)(2,1)} %bitcast.57), calls=%async_computation.3 | async-start | bytes 3145728 | tf_op jit(solution)/shard_map/all_to_all | solution.py:173
  430.2 18.9 %all-to-all-done.2 = bf16[32,24,1024]{2,1,0:T(8,128)(2,1)S(1)} async-done(((bf16[32,24,1024]{2,1,0:T(8,128)(2,1)}), bf16[32,24,1024]{2,1,0:T(8,128)(2,1)S(1)}, u32[]{:S(2)}, u32[]{:S(2)}) %all-to-all-start.2) | async-done | bytes 1572896 | tf_op jit(solution)/shard_map/all_to_all | solution.py:173
  450.3 4.6 convolution_convert_fusion.1
  454.9 7.0 %convolution_convert_fusion.2 = bf16[1024,704]{0,1:T(8,128)(2,1)} fusion(bf16[768,1024]{1,0:T(8,128)(2,1)S(1)} %bitcast.60, f32[768,704]{0,1:T(8,128)} %copy-done.17, bf16[768,1024]{1,0:T(8,128)(2,1)} %bitcast.62, bf16[1,1024,704]{2,1,0:T(8,128)(2,1)} %all-gather.7.cloned.1.call-done), kind=kOutput, calls=%fused_computation.12 | convolution fusion | flops 2220179456 | bytes 8192000 | tf_op jit(solution)/shard_map/dot_general | solution.py:187
  464.0 2.9 copy.45
  467.8 56.4 %psum.38 = bf16[64]{0:T(256)(128)(2,1)S(1)} all-reduce(bf16[64]{0:T(256)(128)(2,1)S(1)} %multiply_reduce_fusion.3), channel_id=1, replica_groups=mesh['dp'=16,'expert'=32] {'expert'}, use_global_device_ids=true, to_apply=%region_22.23 | all-reduce | flops 64 | bytes 256 | tf_op jit(solution)/shard_map/psum | solution.py:150
  525.3 36.0 %all-reduce.6.cloned.1.call-done = bf16[64,1024]{1,0:T(8,128)(2,1)} async-done(((bf16[64,1024]{1,0:T(8,128)(2,1)}), bf16[64,1024]{1,0:T(8,128)(2,1)}) %all-reduce.6.cloned.1.call-update) | async-done | bytes 131088 | tf_op jit(solution)/shard_map/psum | solution.py:149
  563.0 76.8 %reduce-scatter.7.cloned.1.call-done = bf16[64,1408]{1,0:T(8,128)(2,1)} async-done(((bf16[1024,1408]{1,0:T(8,128)(2,1)}), bf16[64,1408]{1,0:T(8,128)(2,1)}) %reduce-scatter.7.cloned.1.call-update) | async-done | bytes 180240
  (148 shorter events, 42.6 us)
Async XLA Ops:
  7.2 250.9 %copy-start = (bf16[64,1024]{1,0:T(8,128)(2,1)S(1)}, bf16[64,1024]{1,0:T(8,128)(2,1)}, u32[]{:S(2)}) copy-start(bf16[64,1024]{1,0:T(8,128)(2,1)} %param.18) | copy-start | bytes 393220
  7.2 79.4 %all-gather.5.cloned.1.call-start = ((), (), s32[]{:S(2)}) async-start(), calls=%async_computation.7 | async-start | bytes 1671168 | tf_op jit(solution)/shard_map/all_gather | solution.py:61
  7.9 150.2 %all-gather.7.cloned.1.call-start = ((), (), s32[]{:S(2)}) async-start(), calls=%async_computation.8 | async-start | bytes 1671168 | tf_op jit(solution)/shard_map/all_gather | solution.py:67
  89.8 72.5 %copy-start.17 = (f32[768,704]{0,1:T(8,128)}, f32[768,704]{0,1:T(8,128)S(1)}, u32[]{:S(2)}) copy-start(f32[768,704]{0,1:T(8,128)S(1)} %fusion.2) | copy-start | bytes 6488068
  162.3 27.7 %all-to-all-start.1 = ((bf16[32,24,1024]{2,1,0:T(8,128)(2,1)}), bf16[32,24,1024]{2,1,0:T(8,128)(2,1)S(1)}, u32[]{:S(2)}, u32[]{:S(2)}) async-start(bf16[32,24,1024]{2,1,0:T(8,128)(2,1)} %bitcast.63), calls=%async_computation.1 | async-start | bytes 3145728 | tf_op jit(solution)/shard_map/all_to_all | solution.py:71
  169.8 242.2 %reduce-scatter.5.cloned.1.call-start = ((), (), s32[]{:S(2)}) async-start(), calls=%async_computation.5 | async-start | bytes 557056 | tf_op jit(solution)/shard_map/reduce_scatter | solution.py:152
  194.4 53.6 %copy-start.13 = (f32[32]{0:T(128)S(1)}, f32[32]{0:T(128)}, u32[]{:S(2)}) copy-start(f32[32]{0:T(128)} %param.25) | copy-start | bytes 388
  194.5 53.6 %copy-start.14 = (s32[1,16]{1,0:T(1,128)S(1)}, s32[1,16]{1,0:T(1,128)}, u32[]{:S(2)}) copy-start(s32[1,16]{1,0:T(1,128)} %param.23) | copy-start | bytes 196
  194.5 53.6 %copy-start.15 = (f32[32]{0:T(128)S(1)}, f32[32]{0:T(128)}, u32[]{:S(2)}) copy-start(f32[32]{0:T(128)} %param.24) | copy-start | bytes 388
  194.5 53.8 %copy-start.12 = (u32[512]{0:T(512)S(1)}, u32[512]{0:T(512)}, u32[]{:S(2)}) copy-start(u32[512]{0:T(512)} %constant.95) | copy-start | bytes 6148
  196.0 62.1 %copy-start.8 = (f32[64]{0:T(128)S(1)}, f32[64]{0:T(128)}, u32[]{:S(2)}) copy-start(f32[64]{0:T(128)} %param.19) | copy-start | bytes 772
  196.4 92.5 %copy-start.16 = (s32[1,16]{1,0:T(1,128)S(1)}, s32[1,16]{1,0:T(1,128)}, u32[]{:S(2)}) copy-start(s32[1,16]{1,0:T(1,128)} %param.22) | copy-start | bytes 196
  196.4 92.6 %copy-start.10 = (s32[1,16]{1,0:T(1,128)S(1)}, s32[1,16]{1,0:T(1,128)}, u32[]{:S(2)}) copy-start(s32[1,16]{1,0:T(1,128)} %param.21) | copy-start | bytes 196
  196.4 7.2 %collective-permute-start = (bf16[16,1024]{1,0:T(8,128)(2,1)S(1)}, bf16[16,1024]{1,0:T(8,128)(2,1)S(1)}, u32[]{:S(2)}, u32[]{:S(2)}) collective-permute-start(bf16[16,1024]{1,0:T(8,128)(2,1)S(1)} %fusion.4), channel_id=1, source_target_pairs={{0,32},{32,64},{64,96},{96,128},{128,160},{160,192},{192,224},{224... | collective-permute-start | bytes 98312 | tf_op jit(solution)/shard_map/ppermute | solution.py:101
  203.6 7.1 %collective-permute-start.1 = (bf16[16,1024]{1,0:T(8,128)(2,1)S(1)}, bf16[16,1024]{1,0:T(8,128)(2,1)S(1)}, u32[]{:S(2)}, u32[]{:S(2)}) collective-permute-start(bf16[16,1024]{1,0:T(8,128)(2,1)S(1)} %collective-permute-done), channel_id=1, source_target_pairs={{0,32},{32,64},{64,96},{96,128},{128,160},{160,192},{192,224},{224... | collective-permute-start | bytes 98312 | tf_op jit(solution)/shard_map/ppermute | solution.py:101
  205.7 6.9 %collective-permute-start.8 = (bf16[16,1024]{1,0:T(8,128)(2,1)S(1)}, bf16[16,1024]{1,0:T(8,128)(2,1)S(1)}, u32[]{:S(2)}, u32[]{:S(2)}) collective-permute-start(bf16[16,1024]{1,0:T(8,128)(2,1)S(1)} %fusion.4), channel_id=1, source_target_pairs={{0,480},{32,0},{64,32},{96,64},{128,96},{160,128},{192,160},{224,1... | collective-permute-start | bytes 98312 | tf_op jit(solution)/shard_map/ppermute | solution.py:105
  210.7 7.1 %collective-permute-start.2 = (bf16[16,1024]{1,0:T(8,128)(2,1)S(1)}, bf16[16,1024]{1,0:T(8,128)(2,1)S(1)}, u32[]{:S(2)}, u32[]{:S(2)}) collective-permute-start(bf16[16,1024]{1,0:T(8,128)(2,1)S(1)} %collective-permute-done.1), channel_id=1, source_target_pairs={{0,32},{32,64},{64,96},{96,128},{128,160},{160,192},{192,224},{224... | collective-permute-start | bytes 98312 | tf_op jit(solution)/shard_map/ppermute | solution.py:101
  212.6 7.1 %collective-permute-start.9 = (bf16[16,1024]{1,0:T(8,128)(2,1)S(1)}, bf16[16,1024]{1,0:T(8,128)(2,1)S(1)}, u32[]{:S(2)}, u32[]{:S(2)}) collective-permute-start(bf16[16,1024]{1,0:T(8,128)(2,1)S(1)} %collective-permute-done.8), channel_id=1, source_target_pairs={{0,480},{32,0},{64,32},{96,64},{128,96},{160,128},{192,160},{224,1... | collective-permute-start | bytes 98312 | tf_op jit(solution)/shard_map/ppermute | solution.py:105
  217.7 7.1 %collective-permute-start.3 = (bf16[16,1024]{1,0:T(8,128)(2,1)S(1)}, bf16[16,1024]{1,0:T(8,128)(2,1)S(1)}, u32[]{:S(2)}, u32[]{:S(2)}) collective-permute-start(bf16[16,1024]{1,0:T(8,128)(2,1)S(1)} %collective-permute-done.2), channel_id=1, source_target_pairs={{0,32},{32,64},{64,96},{96,128},{128,160},{160,192},{192,224},{224... | collective-permute-start | bytes 98312 | tf_op jit(solution)/shard_map/ppermute | solution.py:101
  219.7 7.1 %collective-permute-start.10 = (bf16[16,1024]{1,0:T(8,128)(2,1)S(1)}, bf16[16,1024]{1,0:T(8,128)(2,1)S(1)}, u32[]{:S(2)}, u32[]{:S(2)}) collective-permute-start(bf16[16,1024]{1,0:T(8,128)(2,1)S(1)} %collective-permute-done.9), channel_id=1, source_target_pairs={{0,480},{32,0},{64,32},{96,64},{128,96},{160,128},{192,160},{224,1... | collective-permute-start | bytes 98312 | tf_op jit(solution)/shard_map/ppermute | solution.py:105
  224.8 7.1 %collective-permute-start.4 = (bf16[16,1024]{1,0:T(8,128)(2,1)S(1)}, bf16[16,1024]{1,0:T(8,128)(2,1)S(1)}, u32[]{:S(2)}, u32[]{:S(2)}) collective-permute-start(bf16[16,1024]{1,0:T(8,128)(2,1)S(1)} %collective-permute-done.3), channel_id=1, source_target_pairs={{0,32},{32,64},{64,96},{96,128},{128,160},{160,192},{192,224},{224... | collective-permute-start | bytes 98312 | tf_op jit(solution)/shard_map/ppermute | solution.py:101
  226.8 7.1 %collective-permute-start.11 = (bf16[16,1024]{1,0:T(8,128)(2,1)S(1)}, bf16[16,1024]{1,0:T(8,128)(2,1)S(1)}, u32[]{:S(2)}, u32[]{:S(2)}) collective-permute-start(bf16[16,1024]{1,0:T(8,128)(2,1)S(1)} %collective-permute-done.10), channel_id=1, source_target_pairs={{0,480},{32,0},{64,32},{96,64},{128,96},{160,128},{192,160},{224,1... | collective-permute-start | bytes 98312 | tf_op jit(solution)/shard_map/ppermute | solution.py:105
  231.9 7.1 %collective-permute-start.5 = (bf16[16,1024]{1,0:T(8,128)(2,1)S(1)}, bf16[16,1024]{1,0:T(8,128)(2,1)S(1)}, u32[]{:S(2)}, u32[]{:S(2)}) collective-permute-start(bf16[16,1024]{1,0:T(8,128)(2,1)S(1)} %collective-permute-done.4), channel_id=1, source_target_pairs={{0,32},{32,64},{64,96},{96,128},{128,160},{160,192},{192,224},{224... | collective-permute-start | bytes 98312 | tf_op jit(solution)/shard_map/ppermute | solution.py:101
  233.9 7.1 %collective-permute-start.12 = (bf16[16,1024]{1,0:T(8,128)(2,1)S(1)}, bf16[16,1024]{1,0:T(8,128)(2,1)S(1)}, u32[]{:S(2)}, u32[]{:S(2)}) collective-permute-start(bf16[16,1024]{1,0:T(8,128)(2,1)S(1)} %collective-permute-done.11), channel_id=1, source_target_pairs={{0,480},{32,0},{64,32},{96,64},{128,96},{160,128},{192,160},{224,1... | collective-permute-start | bytes 98312 | tf_op jit(solution)/shard_map/ppermute | solution.py:105
  239.0 7.1 %collective-permute-start.6 = (bf16[16,1024]{1,0:T(8,128)(2,1)S(1)}, bf16[16,1024]{1,0:T(8,128)(2,1)S(1)}, u32[]{:S(2)}, u32[]{:S(2)}) collective-permute-start(bf16[16,1024]{1,0:T(8,128)(2,1)S(1)} %collective-permute-done.5), channel_id=1, source_target_pairs={{0,32},{32,64},{64,96},{96,128},{128,160},{160,192},{192,224},{224... | collective-permute-start | bytes 98312 | tf_op jit(solution)/shard_map/ppermute | solution.py:101
  241.0 9.2 %collective-permute-start.13 = (bf16[16,1024]{1,0:T(8,128)(2,1)S(1)}, bf16[16,1024]{1,0:T(8,128)(2,1)S(1)}, u32[]{:S(2)}, u32[]{:S(2)}) collective-permute-start(bf16[16,1024]{1,0:T(8,128)(2,1)S(1)} %collective-permute-done.12), channel_id=1, source_target_pairs={{0,480},{32,0},{64,32},{96,64},{128,96},{160,128},{192,160},{224,1... | collective-permute-start | bytes 98312 | tf_op jit(solution)/shard_map/ppermute | solution.py:105
  246.1 9.2 %collective-permute-start.7 = (bf16[16,1024]{1,0:T(8,128)(2,1)S(1)}, bf16[16,1024]{1,0:T(8,128)(2,1)S(1)}, u32[]{:S(2)}, u32[]{:S(2)}) collective-permute-start(bf16[16,1024]{1,0:T(8,128)(2,1)S(1)} %collective-permute-done.6), channel_id=1, source_target_pairs={{0,32},{32,64},{64,96},{96,128},{128,160},{160,192},{192,224},{224... | collective-permute-start | bytes 98312 | tf_op jit(solution)/shard_map/ppermute | solution.py:101
  250.2 6.7 %collective-permute-start.14 = (bf16[16,1024]{1,0:T(8,128)(2,1)S(1)}, bf16[16,1024]{1,0:T(8,128)(2,1)S(1)}, u32[]{:S(2)}, u32[]{:S(2)}) collective-permute-start(bf16[16,1024]{1,0:T(8,128)(2,1)S(1)} %collective-permute-done.13), channel_id=1, source_target_pairs={{0,480},{32,0},{64,32},{96,64},{128,96},{160,128},{192,160},{224,1... | collective-permute-start | bytes 98312 | tf_op jit(solution)/shard_map/ppermute | solution.py:105
  258.4 170.6 %copy-start.6 = (f32[256,64]{0,1:T(8,128)}, f32[256,64]{0,1:T(8,128)S(1)}, u32[]{:S(2)}) copy-start(f32[256,64]{0,1:T(8,128)S(1)} %get-tuple-element.43) | copy-start | bytes 196612
  421.3 27.7 %all-to-all-start.2 = ((bf16[32,24,1024]{2,1,0:T(8,128)(2,1)}), bf16[32,24,1024]{2,1,0:T(8,128)(2,1)S(1)}, u32[]{:S(2)}, u32[]{:S(2)}) async-start(bf16[32,24,1024]{2,1,0:T(8,128)(2,1)} %bitcast.57), calls=%async_computation.3 | async-start | bytes 3145728 | tf_op jit(solution)/shard_map/all_to_all | solution.py:173
  428.9 132.4 %all-reduce.6.cloned.1.call-start = ((), (), s32[]{:S(2)}) async-start(), calls=%async_computation.6 | async-start | bytes 262144 | tf_op jit(solution)/shard_map/psum | solution.py:149
  429.9 209.9 %reduce-scatter.7.cloned.1.call-start = ((), (), s32[]{:S(2)}) async-start(), calls=%async_computation.9 | async-start | bytes 3063808
  (8 other events, 32.4 us)
Sparse Core Ops, SparseCore 0:
  10.1 76.4 all-gather.4
  88.6 69.4 all-gather.6
  346.8 65.1 reduce-scatter.4
  433.6 127.7 all-reduce.5
  564.0 75.7 reduce-scatter.6
